TPU v7x, 256 devices: a whole 4x4x8 slice. The times are simulated.
256 devices in a mesh: row: 16 (over y, x), col: 16 (over z, core).
Axes of the slice: x: 4, y: 4, z: 8, core: 2. Of those that a mesh axis runs over, the one named last changes fastest.
Arguments:
- block_input: bfloat16 [512, 12288], P('col', 'row'), may hold values from -6 to 6
- out_grad: bfloat16 [512, 12288], P('col', 'row'), may hold values from -6 to 6
- up_weight: bfloat16 [12288, 24576], P('row', 'col'), may hold values from -0.0546875 to 0.0546875
- down_weight: bfloat16 [24576, 12288], P('col', 'row'), may hold values from -0.0390625 to 0.0390625
Outputs:
- block_output: bfloat16 [512, 12288], P('col', 'row')
- input_grad: bfloat16 [512, 12288], P('col', 'row')
- up_grad: bfloat16 [12288, 24576], P('row', 'col')
- down_grad: bfloat16 [24576, 12288], P('col', 'row')
All inputs are finite; a program needn't handle non-finite values.
Results may differ from a plain program's by a relative error of at most 0.033.
Values may be sent and summed in bfloat16 or wider, within the bound.
A program may use at most 64 MiB of HBM per device.

v0:
```python
import jax
import jax.numpy as jnp
from jax import lax
from jax.sharding import PartitionSpec as P

gelu_c = 0.7978845608028654


def activate(summed, width):
    preact = summed[:, :width]
    hgrad = summed[:, width:]
    cubed = preact * preact * preact
    tanh_term = jnp.tanh(gelu_c * (preact + 0.044715 * cubed))
    value = 0.5 * preact * (1.0 + tanh_term)
    slope = 0.5 * (1.0 + tanh_term) + 0.5 * preact * (1.0 - tanh_term * tanh_term) * gelu_c * (
        1.0 + 3.0 * 0.044715 * preact * preact
    )
    return (value.astype(jnp.bfloat16), (hgrad * slope).astype(jnp.bfloat16))


def body(block_input, out_grad, up_weight, down_weight):
    input_all, grad_all_in = (
        lax.all_gather(block_input, "col", axis=0, tiled=True),
        lax.all_gather(out_grad, "col", axis=0, tiled=True),
    )
    width = up_weight.shape[1]
    model_cols = block_input.shape[1]
    contract_last = (((1,), (1,)), ((), ()))
    contract_first = (((0,), (0,)), ((), ()))
    forward = jnp.dot(input_all, up_weight, preferred_element_type=jnp.float32)
    backward = lax.dot_general(
        grad_all_in, down_weight, contract_last, preferred_element_type=jnp.float32
    )
    summed = lax.psum_scatter(
        jnp.concatenate([forward, backward], axis=1).astype(jnp.bfloat16),
        "row",
        scatter_dimension=0,
        tiled=True,
    ).astype(jnp.float32)
    hidden, act_grad = activate(summed, width)
    hidden_all, act_all = (
        lax.all_gather(hidden, "row", axis=0, tiled=True),
        lax.all_gather(act_grad, "row", axis=0, tiled=True),
    )
    out_part = jnp.dot(hidden_all, down_weight, preferred_element_type=jnp.float32)
    back_part = lax.dot_general(
        act_all, up_weight, contract_last, preferred_element_type=jnp.float32
    )
    combined = lax.psum_scatter(
        jnp.concatenate([out_part, back_part], axis=1).astype(jnp.bfloat16),
        "col",
        scatter_dimension=0,
        tiled=True,
    ).astype(jnp.float32)
    block_output = combined[:, :model_cols].astype(jnp.bfloat16)
    input_grad = combined[:, model_cols:].astype(jnp.bfloat16)
    up_grad = lax.dot_general(
        input_all, act_all, contract_first, preferred_element_type=jnp.float32
    ).astype(jnp.bfloat16)
    down_grad = lax.dot_general(
        hidden_all, grad_all_in, contract_first, preferred_element_type=jnp.float32
    ).astype(jnp.bfloat16)
    return (block_output, input_grad, up_grad, down_grad)


def solution(mesh):
    return jax.shard_map(
        body,
        mesh=mesh,
        in_specs=(P("col", "row"), P("col", "row"), P("row", "col"), P("col", "row")),
        out_specs=(P("col", "row"), P("col", "row"), P("row", "col"), P("col", "row")),
        check_vma=False,
    )
```

profile of v0, /device:TPU:1, one launch (start us, length us, event | category | flops | bytes accessed | tf_op | source)
XLA Modules:
  0.0 303.9 jit_solution(16721811073268089913)
XLA Ops:
  7.2 0.0 copy-start
  7.2 0.0 reduce-scatter.3.cloned.1.call-start
  7.2 23.9 %all_gather.13 = bf16[512,768]{1,0:T(8,128)(2,1)S(1)} all-gather(bf16[32,768]{1,0:T(8,128)(2,1)} %param.5), channel_id=1, replica_groups=mesh['row'=16,'col'=16] {'col'}, dimensions={0}, use_global_device_ids=true | all-gather | bytes 835584 | tf_op jit(solution)/shard_map/all_gather | solution.py:24
  31.1 16.9 %all_gather.12 = bf16[512,768]{1,0:T(8,128)(2,1)S(1)} all-gather(bf16[32,768]{1,0:T(8,128)(2,1)} %param.4), channel_id=1, replica_groups=mesh['row'=16,'col'=16] {'col'}, dimensions={0}, use_global_device_ids=true | all-gather | bytes 835584 | tf_op jit(solution)/shard_map/all_gather | solution.py:23
  47.9 0.0 copy-start.1
  47.9 3.4 %convolution_convert_fusion.2 = bf16[512,1536]{1,0:T(8,128)(2,1)S(1)} fusion(bf16[512,768]{1,0:T(8,128)(2,1)S(1)} %all_gather.13, bf16[1536,768]{1,0:T(8,128)(2,1)} %param.7), kind=kOutput, calls=%fused_computation.4 | convolution fusion | flops 1208745984 | bytes 4718592 | tf_op jit(solution)/shard_map/dot_general | solution.py:31
  51.3 0.0 copy-done.1
  51.3 0.0 copy-done
  51.3 1.4 convolution_convert_fusion.3
  52.7 2.0 pad_maximum_fusion
  54.7 0.0 reduce-scatter.3.cloned.1.call-update
  54.8 0.0 all-gather.5.cloned.1.call-start
  54.8 77.6 %reduce-scatter.3.cloned.1.call-done = bf16[32,3072]{1,0:T(8,128)(2,1)} async-done(((bf16[512,3072]{1,0:T(8,128)(2,1)}), bf16[32,3072]{1,0:T(8,128)(2,1)}) %reduce-scatter.3.cloned.1.call-update) | async-done | bytes 196624 | tf_op jit(solution)/shard_map/reduce_scatter | solution.py:34
  132.4 1.0 convert_element_type.23
  133.3 0.8 multiply_convert_fusion
  134.1 0.0 all-gather.5.cloned.1.call-update
  134.2 0.0 all-gather.3.cloned.1.call-start
  134.2 0.7 all-gather.3.cloned.1.call-update
  134.9 0.0 reduce-scatter.5.cloned.1.call-start
  134.9 49.5 %all-gather.5.cloned.1.call-done = bf16[512,1536]{1,0:T(8,128)(2,1)} async-done(((bf16[32,1536]{1,0:T(8,128)(2,1)}), bf16[512,1536]{1,0:T(8,128)(2,1)}) %all-gather.5.cloned.1.call-update) | async-done | bytes 1572880 | tf_op jit(solution)/shard_map/all_gather | solution.py:43
  184.4 3.7 %convolution_convert_fusion.4 = bf16[512,768]{1,0:T(8,128)(2,1)} fusion(bf16[512,1536]{1,0:T(8,128)(2,1)} %all-gather.5.cloned.1.call-done, bf16[768,1536]{1,0:T(8,128)(2,1)S(1)} %copy-done), kind=kOutput, calls=%fused_computation.7 | convolution fusion | flops 1208352768 | bytes 4718592 | tf_op jit(solution)/shard_map/dot_general | solution.py:46
  188.1 47.1 %all-gather.3.cloned.1.call-done = bf16[512,1536]{1,0:T(8,128)(2,1)} async-done(((bf16[32,1536]{1,0:T(8,128)(2,1)}), bf16[512,1536]{1,0:T(8,128)(2,1)}) %all-gather.3.cloned.1.call-update) | async-done | bytes 1572880 | tf_op jit(solution)/shard_map/all_gather | solution.py:42
  235.2 0.0 copy-start.2
  235.2 3.6 %convolution_convert_fusion.5 = bf16[512,768]{1,0:T(8,128)(2,1)S(1)} fusion(bf16[512,1536]{1,0:T(8,128)(2,1)} %all-gather.3.cloned.1.call-done, bf16[1536,768]{1,0:T(8,128)(2,1)} %param.7), kind=kOutput, calls=%fused_computation.8 | convolution fusion | flops 1208352768 | bytes 4718592 | tf_op jit(solution)/shard_map/dot_general | solution.py:45
  238.8 0.0 copy-done.2
  238.9 1.3 pad_maximum_fusion.1
  240.1 0.0 reduce-scatter.5.cloned.1.call-update
  240.1 4.4 %fusion = bf16[768,1536]{0,1:T(8,128)(2,1)} fusion(bf16[512,1536]{1,0:T(8,128)(2,1)} %all-gather.5.cloned.1.call-done, bf16[512,768]{1,0:T(8,128)(2,1)} %copy-done.1), kind=kOutput, calls=%fused_computation.3 | convolution fusion | flops 1209139200 | bytes 4718592 | tf_op jit(solution)/shard_map/dot_general | solution.py:57
  244.6 4.3 %copy.8 = bf16[768,1536]{1,0:T(8,128)(2,1)} copy(bf16[768,1536]{0,1:T(8,128)(2,1)} %fusion) | data formatting | bytes 4718592
  248.8 4.2 %convolution_convert_fusion = bf16[1536,768]{1,0:T(8,128)(2,1)} fusion(bf16[512,1536]{1,0:T(8,128)(2,1)} %all-gather.3.cloned.1.call-done, bf16[512,768]{1,0:T(8,128)(2,1)S(1)} %all_gather.13), kind=kOutput, calls=%fused_computation | convolution fusion | flops 1209139200 | bytes 4718592 | tf_op jit(solution)/shard_map/dot_general | solution.py:60
  253.1 42.9 %reduce-scatter.5.cloned.1.call-done = bf16[32,1536]{1,0:T(8,128)(2,1)} async-done(((bf16[512,1536]{1,0:T(8,128)(2,1)}), bf16[32,1536]{1,0:T(8,128)(2,1)}) %reduce-scatter.5.cloned.1.call-update) | async-done | bytes 98320 | tf_op jit(solution)/shard_map/reduce_scatter | solution.py:49
  295.9 1.5 fusion.10
Async XLA Ops:
  7.2 44.2 %copy-start = (bf16[768,1536]{1,0:T(8,128)(2,1)S(1)}, bf16[768,1536]{1,0:T(8,128)(2,1)}, u32[]{:S(2)}) copy-start(bf16[768,1536]{1,0:T(8,128)(2,1)} %param.6) | copy-start | bytes 7077892
  7.2 125.2 %reduce-scatter.3.cloned.1.call-start = ((), (), s32[]{:S(2)}) async-start(), calls=%async_computation.2 | async-start | bytes 3342336 | tf_op jit(solution)/shard_map/reduce_scatter | solution.py:34
  47.9 3.4 %copy-start.1 = (bf16[512,768]{1,0:T(8,128)(2,1)}, bf16[512,768]{1,0:T(8,128)(2,1)S(1)}, u32[]{:S(2)}) copy-start(bf16[512,768]{1,0:T(8,128)(2,1)S(1)} %all_gather.12) | copy-start | bytes 2359300
  54.8 129.6 %all-gather.5.cloned.1.call-start = ((), (), s32[]{:S(2)}) async-start(), calls=%async_computation.4 | async-start | bytes 1671168 | tf_op jit(solution)/shard_map/all_gather | solution.py:43
  134.2 101.1 %all-gather.3.cloned.1.call-start = ((), (), s32[]{:S(2)}) async-start(), calls=%async_computation.3 | async-start | bytes 1671168 | tf_op jit(solution)/shard_map/all_gather | solution.py:42
  134.9 161.1 %reduce-scatter.5.cloned.1.call-start = ((), (), s32[]{:S(2)}) async-start(), calls=%async_computation.5 | async-start | bytes 1671168 | tf_op jit(solution)/shard_map/reduce_scatter | solution.py:49
  235.2 3.6 %copy-start.2 = (bf16[512,768]{1,0:T(8,128)(2,1)S(1)}, bf16[512,768]{1,0:T(8,128)(2,1)}, u32[]{:S(2)}) copy-start(bf16[512,768]{1,0:T(8,128)(2,1)} %convolution_convert_fusion.4) | copy-start | bytes 2359300
Sparse Core Ops, SparseCore 0:
  54.9 77.4 reduce-scatter.2
  135.4 48.9 all-gather.4
  186.8 48.3 all-gather.2
  240.3 55.6 reduce-scatter.4
where the time goes:
time: 307 us; the launch traced here: 304 us
  waiting for transfers between devices  218 us (71%)
  blocking collectives  40.7 us (13%)
  matrix products  20.7 us (7%)
  between operations  13.8 us (4%)
  local copies, waits for them, and re-layouts  5.75 us (2%)
  other arithmetic  5.03 us (2%)
    reduce_scatter x1, waiting for transfers between devices, body(): lax.psum_scatter(jnp.concatenate([forward, backward], axis=1).astype(jnp....  77.6 us
    all_gather x1, waiting for transfers between devices, body(): lax.all_gather(act_grad, 'row', axis=0, tiled=True)  49.5 us
    all_gather x1, waiting for transfers between devices, body(): lax.all_gather(hidden, 'row', axis=0, tiled=True)  47.1 us
    reduce_scatter x1, waiting for transfers between devices, body(): lax.psum_scatter(jnp.concatenate([out_part, back_part], axis=1).astype(jn...  42.9 us
    all_gather x1, blocking collectives, body(): lax.all_gather(out_grad, 'col', axis=0, tiled=True)  23.9 us
    all_gather x1, blocking collectives, body(): lax.all_gather(block_input, 'col', axis=0, tiled=True)  16.9 us
  transfers between devices with their start and end apart: 4, of which 4 were waited for; matrix products, arithmetic and copies ran while one was open for 5% of the time, Pallas kernels for 0%

commit v1 on v0

v1 whole, which is shorter than its diff:
```python
import functools

import jax
import jax.numpy as jnp
from jax import lax
from jax.experimental import pallas as pl
from jax.experimental.pallas import tpu as pltpu
from jax.sharding import PartitionSpec as P

MESH = pl.DeviceIdType.MESH
gelu_c = 0.7978845608028654
f32 = jnp.float32
bf16 = jnp.bfloat16

NX = 4
NZ = 8
ORDER = (1, -1, 2, -2, 3, -3, 0, 4)
POS = {d: i for i, d in enumerate(ORDER)}
CHUNKS = ((0, 1), (2, 3), (4, 5), (6, 7))
STEP = 1
N_SEMS = 224


def activate(preact, hgrad):
    cubed = preact * preact * preact
    tanh_term = jnp.tanh(gelu_c * (preact + 0.044715 * cubed))
    value = 0.5 * preact * (1.0 + tanh_term)
    slope = 0.5 * (1.0 + tanh_term) + 0.5 * preact * (1.0 - tanh_term * tanh_term) * gelu_c * (
        1.0 + 3.0 * 0.044715 * preact * preact
    )
    return value.astype(bf16), (hgrad * slope).astype(bf16)


def dot(a, b, ca, cb):
    return lax.dot_general(a, b, (((ca,), (cb,)), ((), ())), preferred_element_type=f32)


def kernel(
    x_in, g_in, u_in, d_in,
    out_o, back_o, ug_o, dg_o,
    xg, u, dn, part, hid, via, full, quarter, got, outp, sib, zbuf, small, ug, dg,
    ssem, rsem, lsem,
):
    tb, dk = x_in.shape
    fq = u.shape[2]
    st = 2 * tb
    sub = st // NX
    row, col = lax.axis_index("row"), lax.axis_index("col")
    cx, cy = row % NX, row // NX
    cz, core = col // 2, col % 2

    def device(axis, off):
        if axis == "x":
            return (cy * NX + (cx + off) % NX, col)
        if axis == "y":
            return (((cy + off) % NX) * NX + cx, col)
        if axis == "z":
            return (row, ((cz + off) % NZ) * 2 + core)
        return (row, cz * 2 + 1 - core)

    place = {"x": cx, "y": cy}
    sends = []
    n_local = [0]

    def send(src, dst, target):
        i = len(sends)
        copy = pltpu.make_async_remote_copy(
            src_ref=src, dst_ref=dst, send_sem=ssem.at[i], recv_sem=rsem.at[i],
            device_id=target, device_id_type=MESH,
        )
        copy.start()
        sends.append(copy)
        return copy

    def local(src, dst):
        i = n_local[0]
        n_local[0] += 1
        copy = pltpu.make_async_copy(src, dst, lsem.at[i])
        copy.start()
        return copy

    def rows(pos, first=0, count=st):
        return pl.ds(pos * st + first, count)

    own = [
        local(x_in, xg.at[rows(POS[0], 0, tb), pl.ds(0, dk)]),
        local(g_in, xg.at[rows(POS[0], 0, tb), pl.ds(dk, dk)]),
    ]
    weights = [local(u_in.at[:, pl.ds(q * fq, fq)], u.at[q]) for q in range(NX)]
    weights += [local(d_in.at[pl.ds(q * fq, fq), :], dn.at[q]) for q in range(NX)]

    barrier = pltpu.get_barrier_semaphore()
    partners = [(a, o) for a in "xy" for o in (1, 2, 3)] + [("z", o) for o in range(1, NZ)] + [("c", 1)]
    for axis, off in partners:
        pl.semaphore_signal(barrier, inc=1, device_id=device(axis, off), device_id_type=MESH)
    pl.semaphore_wait(barrier, len(partners))

    arrival, shared = {}, {}

    def pass_on(d, to, cols=None):
        cols = pl.ds(0, 2 * dk) if cols is None else cols
        return send(xg.at[rows(POS[d], 0, tb), cols], xg.at[rows(POS[to], 0, tb), cols],
                    device("z", 1 if to < 0 or (to == 4 and d < 0) else -1))

    def share(d):
        shared[d] = send(xg.at[rows(POS[d], 0, tb)], xg.at[rows(POS[d], tb, tb)], device("c", 1))

    for copy in own:
        copy.wait()
    arrival[-1] = [pass_on(0, -1)]
    arrival[1] = [pass_on(0, 1)]
    share(0)

    def arrive(d):
        for copy in arrival[d]:
            copy.wait_recv()
        if d in (-1, -2):
            arrival[d - 1] = [pass_on(d, d - 1)]
        elif d in (1, 2):
            arrival[d + 1] = [pass_on(d, d + 1)]
        elif d == -3:
            arrival.setdefault(4, []).append(pass_on(d, 4, pl.ds(0, dk)))
        elif d == 3:
            arrival.setdefault(4, []).append(pass_on(d, 4, pl.ds(dk, dk)))
        share(d)

    pend = {}

    def axes(pos):
        return ("x", "y") if pos % 2 == 0 else ("y", "x")

    def first_products(chunk):
        for pos in chunk:
            shared[ORDER[pos]].wait_recv()
        span = pl.ds(chunk[0] * st, len(chunk) * st)
        xs, gs = xg[span, :dk], xg[span, dk:]

        def one(q, _):
            part[q, span, :fq] = dot(xs, u[q], 1, 0).astype(bf16)
            part[q, span, fq:] = dot(gs, dn[q], 1, 1).astype(bf16)
            return 0

        lax.fori_loop(0, NX, one, 0)
        for pos in chunk:
            a1, _ = axes(pos)
            far = (place[a1] + 2) % NX
            pend[pos] = [
                send(part.at[far, rows(pos), pl.ds(0, fq)], via.at[0, pos], device(a1, 1)),
                send(part.at[far, rows(pos), pl.ds(fq, fq)], via.at[1, pos], device(a1, -1)),
            ]

    def first_sum(chunk):
        for pos in chunk:
            a1, _ = axes(pos)
            right, left = (place[a1] + 1) % NX, (place[a1] + NX - 1) % NX
            pend[pos][0].wait_recv()
            part[right, rows(pos), :fq] = (
                part[right, rows(pos), :fq].astype(f32) + via[0, pos].astype(f32)
            ).astype(bf16)
            to_right = send(part.at[right, rows(pos)], full.at[0, pos], device(a1, 1))
            pend[pos][1].wait_recv()
            part[left, rows(pos), fq:] = (
                part[left, rows(pos), fq:].astype(f32) + via[1, pos].astype(f32)
            ).astype(bf16)
            pend[pos] = [to_right, send(part.at[left, rows(pos)], full.at[1, pos], device(a1, -1))]

    def second_sum(chunk):
        for pos in chunk:
            a1, a2 = axes(pos)
            for copy in pend[pos]:
                copy.wait_recv()
            total = (
                part[place[a1], rows(pos), :].astype(f32) + full[0, pos].astype(f32) + full[1, pos].astype(f32)
            ).astype(bf16)
            for k in range(NX):
                quarter[pos, k] = total[k * sub:(k + 1) * sub]
            pend[pos] = [
                send(quarter.at[pos, (place[a2] + o) % NX], got.at[pos, o - 1], device(a2, o)) for o in (1, 3, 2)
            ]

    def act(chunk):
        for pos in chunk:
            a1, a2 = axes(pos)
            for copy in pend[pos]:
                copy.wait_recv()
            total = quarter[pos, place[a2]].astype(f32)
            for o in range(NX - 1):
                total = total + got[pos, o].astype(f32)
            value, grad = activate(total[:, :fq], total[:, fq:])
            mine = pl.ds(pl.multiple_of(pos * st + place[a2] * sub, sub), sub)
            hid[place[a1], mine, :fq] = value
            hid[place[a1], mine, fq:] = grad
            block = hid.at[place[a1], mine]
            pend[pos] = [send(block, block, device(a2, o)) for o in (1, 3, 2)]

    def gather(chunk):
        for pos in chunk:
            a1, _ = axes(pos)
            for copy in pend[pos]:
                copy.wait_recv()
            block = hid.at[place[a1], rows(pos)]
            pend[pos] = [send(block, block, device(a1, 1)), send(block, block, device(a1, -1))]

    def forward(chunk):
        for pos in chunk:
            a1, _ = axes(pos)
            right, left = (place[a1] + 1) % NX, (place[a1] + NX - 1) % NX
            pend[pos][0].wait_recv()
            block = hid.at[left, rows(pos), pl.ds(0, fq)]
            to_right = send(block, block, device(a1, 1))
            pend[pos][1].wait_recv()
            block = hid.at[right, rows(pos), pl.ds(fq, fq)]
            pend[pos] = [to_right, send(block, block, device(a1, -1))]

    def second_products(chunk):
        for pos in chunk:
            for copy in pend[pos]:
                copy.wait_recv()
        span = pl.ds(chunk[0] * st, len(chunk) * st)
        out = dot(hid[0, span, :fq], dn[0], 1, 0)
        for q in range(1, NX):
            out = out + dot(hid[q, span, :fq], dn[q], 1, 0)
        outp[span, :dk] = out.astype(bf16)
        back = dot(hid[0, span, fq:], u[0], 1, 1)
        for q in range(1, NX):
            back = back + dot(hid[q, span, fq:], u[q], 1, 1)
        outp[span, dk:] = back.astype(bf16)
        for pos in chunk:
            pend[pos] = [send(outp.at[rows(pos, tb, tb)], sib.at[pos], device("c", 1))]

    landed = []

    def both_cores(chunk):
        for pos in chunk:
            pend[pos][0].wait_recv()
            mine = rows(pos, 0, tb)
            outp[mine, :] = (outp[mine, :].astype(f32) + sib[pos].astype(f32)).astype(bf16)
            d = ORDER[pos]
            if d:
                landed.append(send(outp.at[mine], zbuf.at[pos], device("z", d)))

    stages = [first_products, first_sum, second_sum, act, gather, forward, second_products, both_cores]
    for tick in range(len(stages) + STEP * (len(CHUNKS) - 1)):
        for k in range(len(CHUNKS)):
            s = tick - STEP * k
            if s == 0:
                if k == 0:
                    for copy in weights:
                        copy.wait()
                for pos in CHUNKS[k]:
                    if ORDER[pos]:
                        arrive(ORDER[pos])
            if 0 <= s < len(stages):
                stages[s](CHUNKS[k])

    def weight_grads(q, _):
        ug[q] = dot(xg[:, :dk], hid[q, :, fq:], 0, 0).astype(bf16)
        pltpu.make_async_copy(ug.at[q], ug_o.at[:, pl.ds(pl.multiple_of(q * fq, 128), fq)], lsem.at[16 + q]).start()
        dg[q] = dot(hid[q, :, :fq], xg[:, dk:], 0, 0).astype(bf16)
        pltpu.make_async_copy(dg.at[q], dg_o.at[pl.ds(pl.multiple_of(q * fq, 128), fq), :], lsem.at[20 + q]).start()
        return 0

    lax.fori_loop(0, NX, weight_grads, 0)

    for copy in landed:
        copy.wait_recv()
    total = outp[rows(POS[0], 0, tb), :].astype(f32)
    for d in ORDER:
        if d:
            total = total + zbuf[POS[d]].astype(f32)
    small[...] = total.astype(bf16)
    finals = [local(small.at[:, pl.ds(0, dk)], out_o), local(small.at[:, pl.ds(dk, dk)], back_o)]
    for copy in sends:
        copy.wait_send()
    for copy in finals:
        copy.wait()
    for q in range(NX):
        pltpu.make_async_copy(ug.at[q], ug_o.at[:, pl.ds(q * fq, fq)], lsem.at[16 + q]).wait()
        pltpu.make_async_copy(dg.at[q], dg_o.at[pl.ds(q * fq, fq), :], lsem.at[20 + q]).wait()


def body(block_input, out_grad, up_weight, down_weight):
    tb, dk = block_input.shape
    f = up_weight.shape[1]
    fq, st, n = f // NX, 2 * tb, NZ
    anywhere = pl.BlockSpec(memory_space=pl.ANY)
    vm = lambda *shape: pltpu.VMEM(shape, bf16)
    return pl.pallas_call(
        kernel,
        name="block",
        out_shape=(
            jax.ShapeDtypeStruct((tb, dk), bf16),
            jax.ShapeDtypeStruct((tb, dk), bf16),
            jax.ShapeDtypeStruct((dk, f), bf16),
            jax.ShapeDtypeStruct((f, dk), bf16),
        ),
        in_specs=[anywhere] * 4,
        out_specs=(anywhere,) * 4,
        scratch_shapes=[
            vm(n * st, 2 * dk),
            vm(NX, dk, fq),
            vm(NX, fq, dk),
            vm(NX, n * st, 2 * fq),
            vm(NX, n * st, 2 * fq),
            vm(2, n, st, fq),
            vm(2, n, st, 2 * fq),
            vm(n, NX, st // NX, 2 * fq),
            vm(n, NX - 1, st // NX, 2 * fq),
            vm(n * st, 2 * dk),
            vm(n, tb, 2 * dk),
            vm(n, tb, 2 * dk),
            vm(tb, 2 * dk),
            vm(NX, dk, fq),
            vm(NX, fq, dk),
            pltpu.SemaphoreType.DMA((N_SEMS,)),
            pltpu.SemaphoreType.DMA((N_SEMS,)),
            pltpu.SemaphoreType.DMA((24,)),
        ],
        compiler_params=pltpu.CompilerParams(
            collective_id=0, has_side_effects=True, vmem_limit_bytes=56 * 2**20
        ),
        cost_estimate=pl.CostEstimate(flops=12 * n * st * dk * f, bytes_accessed=8 * dk * f, transcendentals=0),
    )(block_input, out_grad, up_weight, down_weight)


def solution(mesh):
    return jax.shard_map(
        body,
        mesh=mesh,
        in_specs=(P("col", "row"), P("col", "row"), P("row", "col"), P("col", "row")),
        out_specs=(P("col", "row"), P("col", "row"), P("row", "col"), P("col", "row")),
        check_vma=False,
    )
```

time: 307 us -> 91.5 us (0.30)
  waiting for transfers between devices: 218 us -> 0 us
  Pallas kernels: 0 us -> 83.1 us
  blocking collectives: 40.7 us -> 0 us
  matrix products: 20.7 us -> 0 us
  between operations: 13.8 us -> 0.64 us
  other arithmetic: 5.03 us -> 0 us
    reduce_scatter x2 -> x0, waiting for transfers between devices: 120 us -> none  [the longest x1 77.6 us: body(): lax.psum_scatter(jnp.concatenate([forward, backward], axis=1).astype(jnp....]
    all_gather x2 -> x0, waiting for transfers between devices: 96.6 us -> none  [the longest x1 49.5 us: body(): lax.all_gather(act_grad, 'row', axis=0, tiled=True)]
    pallas_call x0 -> x1, Pallas kernels: none -> 83.1 us  [body(): pl.pallas_call(kernel, name='block', out_shape=(jax.ShapeDtypeStruct((tb,...]
    all_gather x2 -> x0, blocking collectives: 40.7 us -> none  [the longest x1 23.9 us: body(): lax.all_gather(out_grad, 'col', axis=0, tiled=True)]
    dot_general x6 -> x0, matrix products: 20.7 us -> none  [the longest x1 4.44 us: body(): lax.dot_general(input_all, act_all, contract_first, preferred_element_typ...]
    unnamed x7 -> x6, local copies, waits for them, and re-layouts: 4.28 us -> 7.62 us
    concatenate x2 -> x0, other arithmetic: 3.27 us -> none  [the longest x1 2.01 us: body(): jnp.concatenate([forward, backward], axis=1).astype(jnp.bfloat16)]
  transfers between devices with their start and end apart: 4 -> 0, of which waited for: 4 -> 0; matrix products, arithmetic and copies ran while one was open for 5% -> 0% of each run, Pallas kernels for 0% -> 0%
where the time goes in v1:
time: 91.5 us; the launch traced here: 91.3 us
  Pallas kernels  83.1 us (91%)
  local copies, waits for them, and re-layouts  7.62 us (8%)
    pallas_call x1, Pallas kernels, body(): pl.pallas_call(kernel, name='block', out_shape=(jax.ShapeDtypeStruct((tb,...  83.1 us
    unnamed x6, local copies, waits for them, and re-layouts  7.62 us

profile of v1, /device:TPU:1, one launch (start us, length us, event | category | flops | bytes accessed | tf_op | source)
XLA Modules:
  0.0 91.3 jit_solution(15581746637401963180)
XLA Ops:
  0.6 83.1 %block.1 = (bf16[32,768]{1,0:T(8,128)(2,1)}, bf16[32,768]{1,0:T(8,128)(2,1)}, bf16[768,1536]{1,0:T(8,128)(2,1)}, bf16[1536,768]{1,0:T(8,128)(2,1)}) custom-call(bf16[32,768]{1,0:T(8,128)(2,1)} %x_in.1, bf16[32,768]{1,0:T(8,128)(2,1)} %g_in.1, bf16[768,1536]{1,0:T(8,128)(2,1)} %u_in.1, bf16[1536,768]{1,0:T(8,128)(2,1)} %d_in.1), custom_call_target="tpu_custom_call" | custom-call | flops 7247757312 | bytes 9437184 | tf_op jit(solution)/shard_map/block/pallas_call | solution.py:288
  83.7 1.4 %copy.12 = bf16[32,768]{1,0:T(8,128)(2,1)} copy(bf16[32,768]{1,0:T(8,128)(2,1)} %get-tuple-element.8) | data formatting | bytes 98304
  85.1 1.4 %copy.13 = bf16[32,768]{1,0:T(8,128)(2,1)} copy(bf16[32,768]{1,0:T(8,128)(2,1)} %get-tuple-element.9) | data formatting | bytes 98304
  86.5 0.0 copy-start
  86.6 3.4 %copy.14 = bf16[768,1536]{1,0:T(8,128)(2,1)} copy(bf16[768,1536]{1,0:T(8,128)(2,1)} %get-tuple-element.10) | data formatting | bytes 4718592
  89.9 0.0 copy-done
  89.9 1.4 %copy.15 = bf16[1536,768]{1,0:T(8,128)(2,1)} copy(bf16[1536,768]{1,0:T(8,128)(2,1)S(1)} %copy-done) | data formatting | bytes 4718592
Async XLA Ops:
  86.5 3.4 %copy-start = (bf16[1536,768]{1,0:T(8,128)(2,1)S(1)}, bf16[1536,768]{1,0:T(8,128)(2,1)}, u32[]{:S(2)}) copy-start(bf16[1536,768]{1,0:T(8,128)(2,1)} %get-tuple-element.11) | copy-start | bytes 7077892

commit v2 on v1

v2 whole, which is shorter than its diff:
```python
import functools

import jax
import jax.numpy as jnp
from jax import lax
from jax.experimental import pallas as pl
from jax.experimental.pallas import tpu as pltpu
from jax.sharding import PartitionSpec as P

MESH = pl.DeviceIdType.MESH
gelu_c = 0.7978845608028654
f32 = jnp.float32
bf16 = jnp.bfloat16

NX = 4
NZ = 8
ORDER = (0, 2, -2, 3, -3, 4, 1, -1)
ZSLOT = {1: 0, -1: 1, 2: 2, -2: 3}
POS = {d: i for i, d in enumerate(ORDER)}
CHUNKS = ((0,), (1, 2), (3, 4), (5,), (6, 7))
SCHEDULE = (
    ("p1", 0), ("arr", 1), ("arr", -1), ("p1", 4), ("arr", -2), ("arr", 2), ("s1", 0), ("p1", 1),
    ("arr", -3), ("arr", 3), ("s1", 7), ("s1", 6), ("p1", 2), ("arr", 4), ("s2", 7), ("s1", 1),
    ("p1", 3), ("s1", 4), ("s1", 3), ("s1", 2), ("s2", 6), ("s1", 5), ("s2", 1), ("s3", 7),
    ("s2", 4), ("s2", 3), ("s2", 2), ("s2", 0), ("s3", 6), ("s2", 5), ("s3", 4), ("s4", 7),
    ("s3", 3), ("s3", 1), ("s3", 0), ("s3", 2), ("s3", 5), ("s4", 4), ("s4", 3), ("s4", 6),
    ("s4", 5), ("s5", 4), ("s4", 2), ("s5", 3), ("s5", 5), ("s4", 0), ("s4", 1), ("s5", 7),
    ("s5", 6), ("s5", 2), ("p2", 2), ("p2", 3), ("s6", 3), ("s5", 1), ("s6", 5), ("s6", 4),
    ("s5", 0), ("p2", 4), ("p2", 1), ("s6", 6), ("s6", 7), ("p2", 0), ("s6", 1), ("s6", 2),
    ("s6", 0), ("dw", 0),
)
N_SEMS = 224


def activate(preact, hgrad):
    cubed = preact * preact * preact
    tanh_term = jnp.tanh(gelu_c * (preact + 0.044715 * cubed))
    value = 0.5 * preact * (1.0 + tanh_term)
    slope = 0.5 * (1.0 + tanh_term) + 0.5 * preact * (1.0 - tanh_term * tanh_term) * gelu_c * (
        1.0 + 3.0 * 0.044715 * preact * preact
    )
    return value.astype(bf16), (hgrad * slope).astype(bf16)


def dot(a, b, ca, cb):
    return lax.dot_general(a, b, (((ca,), (cb,)), ((), ())), preferred_element_type=f32)


def kernel(
    x_in, g_in, u_in, d_in,
    out_o, back_o, ug_o, dg_o,
    xg, u, dn, part, hid, via, full, quarter, got, outp, sib, zbuf, mid, mid4, small, ug, dg,
    ssem, rsem, lsem,
):
    tb, dk = x_in.shape
    fq = u.shape[2]
    st = 2 * tb
    sub = st // NX
    row, col = lax.axis_index("row"), lax.axis_index("col")
    cx, cy = row % NX, row // NX
    cz, core = col // 2, col % 2

    def device(axis, off):
        if axis == "x":
            return (cy * NX + (cx + off) % NX, col)
        if axis == "y":
            return (((cy + off) % NX) * NX + cx, col)
        if axis == "z":
            return (row, ((cz + off) % NZ) * 2 + core)
        return (row, cz * 2 + 1 - core)

    place = {"x": cx, "y": cy}
    sends = []
    n_local = [0]

    def send(src, dst, target):
        i = len(sends)
        copy = pltpu.make_async_remote_copy(
            src_ref=src, dst_ref=dst, send_sem=ssem.at[i], recv_sem=rsem.at[i],
            device_id=target, device_id_type=MESH,
        )
        copy.start()
        sends.append(copy)
        return copy

    def local(src, dst):
        i = n_local[0]
        n_local[0] += 1
        copy = pltpu.make_async_copy(src, dst, lsem.at[i])
        copy.start()
        return copy

    def rows(pos, first=0, count=st):
        return pl.ds(pos * st + first, count)

    own = [
        local(x_in, xg.at[rows(POS[0], 0, tb), pl.ds(0, dk)]),
        local(g_in, xg.at[rows(POS[0], 0, tb), pl.ds(dk, dk)]),
    ]
    weights = [local(u_in.at[:, pl.ds(q * fq, fq)], u.at[q]) for q in range(NX)]
    weights += [local(d_in.at[pl.ds(q * fq, fq), :], dn.at[q]) for q in range(NX)]

    barrier = pltpu.get_barrier_semaphore()
    partners = [(a, o) for a in "xy" for o in (1, 2, 3)] + [("z", o) for o in range(1, NZ)] + [("c", 1)]
    for axis, off in partners:
        pl.semaphore_signal(barrier, inc=1, device_id=device(axis, off), device_id_type=MESH)
    pl.semaphore_wait(barrier, len(partners))

    arrival, shared = {}, {}

    def pass_on(d, to, off, cols=None):
        cols = pl.ds(0, 2 * dk) if cols is None else cols
        copy = send(xg.at[rows(POS[d], 0, tb), cols], xg.at[rows(POS[to], 0, tb), cols], device("z", off))
        arrival.setdefault(to, []).append(copy)

    def share(d):
        shared[d] = send(xg.at[rows(POS[d], 0, tb)], xg.at[rows(POS[d], tb, tb)], device("c", 1))

    for copy in own:
        copy.wait()
    pass_on(0, -1, 1)
    pass_on(0, 1, -1)
    share(0)
    pass_on(0, -2, 2)
    pass_on(0, 2, -2)

    def arrive(d):
        for copy in arrival[d]:
            copy.wait_recv()
        if d in (1, -1):
            pass_on(d, 3 * d, -2 * d)
        elif d == -2:
            pass_on(d, 4, 2, pl.ds(0, dk))
        elif d == 2:
            pass_on(d, 4, -2, pl.ds(dk, dk))
        share(d)

    pend, first = {}, {}
    low, high = pl.ds(0, fq), pl.ds(fq, fq)

    def axes(pos):
        return ("x", "y") if pos % 2 == 0 else ("y", "x")

    def first_products(chunk):
        for pos in chunk:
            shared[ORDER[pos]].wait_recv()
        span = pl.ds(chunk[0] * st, len(chunk) * st)
        xs, gs = xg[span, :dk], xg[span, dk:]

        def one(q, _):
            part[q, span, :fq] = dot(xs, u[q], 1, 0).astype(bf16)
            part[q, span, fq:] = dot(gs, dn[q], 1, 1).astype(bf16)
            return 0

        lax.fori_loop(0, NX, one, 0)
        for pos in chunk:
            a1, _ = axes(pos)
            far = (place[a1] + 2) % NX
            right, left = (place[a1] + 1) % NX, (place[a1] + NX - 1) % NX
            first[pos] = [
                send(part.at[far, rows(pos), low], via.at[0, pos], device(a1, 1)),
                send(part.at[far, rows(pos), high], via.at[1, pos], device(a1, -1)),
            ]
            pend[pos] = [
                send(part.at[right, rows(pos), high], full.at[0, pos, :, high], device(a1, 1)),
                send(part.at[left, rows(pos), low], full.at[1, pos, :, low], device(a1, -1)),
            ]

    def first_sum(pos):
        a1, _ = axes(pos)
        right, left = (place[a1] + 1) % NX, (place[a1] + NX - 1) % NX
        first[pos][0].wait_recv()
        part[right, rows(pos), :fq] = (
            part[right, rows(pos), :fq].astype(f32) + via[0, pos].astype(f32)
        ).astype(bf16)
        pend[pos].append(send(part.at[right, rows(pos), low], full.at[0, pos, :, low], device(a1, 1)))
        first[pos][1].wait_recv()
        part[left, rows(pos), fq:] = (
            part[left, rows(pos), fq:].astype(f32) + via[1, pos].astype(f32)
        ).astype(bf16)
        pend[pos].append(send(part.at[left, rows(pos), high], full.at[1, pos, :, high], device(a1, -1)))

    def second_sum(pos):
        a1, a2 = axes(pos)
        for copy in pend[pos]:
            copy.wait_recv()
        total = (
            part[place[a1], rows(pos), :].astype(f32) + full[0, pos].astype(f32) + full[1, pos].astype(f32)
        ).astype(bf16)
        for k in range(NX):
            quarter[pos, k] = total[k * sub:(k + 1) * sub]
        pend[pos] = [
            send(quarter.at[pos, (place[a2] + o) % NX], got.at[pos, o - 1], device(a2, o)) for o in (1, 3, 2)
        ]

    def act(pos):
        a1, a2 = axes(pos)
        for copy in pend[pos]:
            copy.wait_recv()
        total = quarter[pos, place[a2]].astype(f32)
        for o in range(NX - 1):
            total = total + got[pos, o].astype(f32)
        value, grad = activate(total[:, :fq], total[:, fq:])
        mine = pl.ds(pl.multiple_of(pos * st + place[a2] * sub, sub), sub)
        hid[place[a1], mine, :fq] = value
        hid[place[a1], mine, fq:] = grad
        block = hid.at[place[a1], mine]
        pend[pos] = [send(block, block, device(a2, o)) for o in (1, 3, 2)]

    def gather(pos):
        a1, _ = axes(pos)
        for copy in pend[pos]:
            copy.wait_recv()
        h = hid.at[place[a1], rows(pos), low]
        a = hid.at[place[a1], rows(pos), high]
        first[pos] = [send(h, h, device(a1, 1)), send(a, a, device(a1, -1))]
        pend[pos] = [send(a, a, device(a1, 1)), send(h, h, device(a1, -1))]

    def forward(pos):
        a1, _ = axes(pos)
        right, left = (place[a1] + 1) % NX, (place[a1] + NX - 1) % NX
        first[pos][0].wait_recv()
        block = hid.at[left, rows(pos), low]
        pend[pos].append(send(block, block, device(a1, 1)))
        first[pos][1].wait_recv()
        block = hid.at[right, rows(pos), high]
        pend[pos].append(send(block, block, device(a1, -1)))

    def second_products(chunk):
        for pos in chunk:
            for copy in pend[pos]:
                copy.wait_recv()
        span = pl.ds(chunk[0] * st, len(chunk) * st)
        out = dot(hid[0, span, :fq], dn[0], 1, 0)
        for q in range(1, NX):
            out = out + dot(hid[q, span, :fq], dn[q], 1, 0)
        outp[span, :dk] = out.astype(bf16)
        back = dot(hid[0, span, fq:], u[0], 1, 1)
        for q in range(1, NX):
            back = back + dot(hid[q, span, fq:], u[q], 1, 1)
        outp[span, dk:] = back.astype(bf16)
        for pos in chunk:
            pend[pos] = [send(outp.at[rows(pos, tb, tb)], sib.at[pos], device("c", 1))]

    landed = []

    def both_cores(pos):
        pend[pos][0].wait_recv()
        mine = rows(pos, 0, tb)
        total = outp[mine, :].astype(f32) + sib[pos].astype(f32)
        d = ORDER[pos]
        if d in (2, -2):
            side = 0 if d > 0 else 1
            far[3 if d > 0 else -3].wait_recv()
            far[4][side].wait_recv()
            total = total + mid[side].astype(f32)
            cols = slice(side * dk, side * dk + dk)
            outp[mine, :] = total.astype(bf16)
            outp[mine, cols] = (total[:, cols] + mid4[side].astype(f32)).astype(bf16)
        else:
            outp[mine, :] = total.astype(bf16)
        if d in (3, -3):
            far[d] = send(outp.at[mine], mid.at[0 if d > 0 else 1], device("z", d // 3))
        elif d == 4:
            far[4] = [
                send(outp.at[mine, pl.ds(0, dk)], mid4.at[0], device("z", 2)),
                send(outp.at[mine, pl.ds(dk, dk)], mid4.at[1], device("z", -2)),
            ]
        elif d:
            landed[d] = send(outp.at[mine], zbuf.at[ZSLOT[d]], device("z", d))

    far, landed = {}, {}

    def weight_grads(q, _):
        ug[q] = dot(xg[:, :dk], hid[q, :, fq:], 0, 0).astype(bf16)
        pltpu.make_async_copy(ug.at[q], ug_o.at[:, pl.ds(pl.multiple_of(q * fq, 128), fq)], lsem.at[16 + q]).start()
        dg[q] = dot(hid[q, :, :fq], xg[:, dk:], 0, 0).astype(bf16)
        pltpu.make_async_copy(dg.at[q], dg_o.at[pl.ds(pl.multiple_of(q * fq, 128), fq), :], lsem.at[20 + q]).start()
        return 0

    def all_weight_grads(_):
        lax.fori_loop(0, NX, weight_grads, 0)

    steps = {
        "arr": arrive, "p1": first_products, "s1": first_sum, "s2": second_sum, "s3": act, "s4": gather,
        "s5": forward, "p2": second_products, "s6": both_cores, "dw": all_weight_grads,
    }
    for copy in weights:
        copy.wait()
    for name, number in SCHEDULE:
        steps[name](CHUNKS[number] if name in ("p1", "p2") else number)

    total = outp[rows(POS[0], 0, tb), :].astype(f32)
    for d in (1, -1, 2, -2):
        landed[d].wait_recv()
        total = total + zbuf[ZSLOT[d]].astype(f32)
    small[...] = total.astype(bf16)
    finals = [local(small.at[:, pl.ds(0, dk)], out_o), local(small.at[:, pl.ds(dk, dk)], back_o)]
    for copy in sends:
        copy.wait_send()
    for copy in finals:
        copy.wait()
    for q in range(NX):
        pltpu.make_async_copy(ug.at[q], ug_o.at[:, pl.ds(q * fq, fq)], lsem.at[16 + q]).wait()
        pltpu.make_async_copy(dg.at[q], dg_o.at[pl.ds(q * fq, fq), :], lsem.at[20 + q]).wait()


CUTS = 4


def settle_kernel(*refs):
    n = (len(refs) - 2) // 3
    sources, results, held = refs[:n], refs[n:2 * n], refs[2 * n:3 * n]
    load_sem, store_sem = refs[-2:]
    moves = []
    for i in range(n):
        count = sources[i].shape[0]
        cuts = CUTS if count > 64 else 1
        for c in range(cuts):
            part = pl.ds(c * (count // cuts), count // cuts)
            load = pltpu.make_async_copy(sources[i].at[part], held[i].at[part], load_sem.at[i, c])
            store = pltpu.make_async_copy(held[i].at[part], results[i].at[part], store_sem.at[i, c])
            load.start()
            moves.append((load, store))
    for load, store in moves:
        load.wait()
        store.start()
    for _, store in moves:
        store.wait()


def settle(*arrays):
    anywhere = pl.BlockSpec(memory_space=pl.ANY)
    n = len(arrays)
    return pl.pallas_call(
        settle_kernel,
        name="settle",
        out_shape=tuple(jax.ShapeDtypeStruct(a.shape, a.dtype) for a in arrays),
        in_specs=[anywhere] * n,
        out_specs=(anywhere,) * n,
        scratch_shapes=[pltpu.VMEM(a.shape, a.dtype) for a in arrays]
        + [pltpu.SemaphoreType.DMA((n, CUTS)), pltpu.SemaphoreType.DMA((n, CUTS))],
        compiler_params=pltpu.CompilerParams(vmem_limit_bytes=56 * 2**20),
    )(*arrays)


def body(block_input, out_grad, up_weight, down_weight):
    tb, dk = block_input.shape
    f = up_weight.shape[1]
    fq, st, n = f // NX, 2 * tb, NZ
    anywhere = pl.BlockSpec(memory_space=pl.ANY)
    vm = lambda *shape: pltpu.VMEM(shape, bf16)
    results = pl.pallas_call(
        kernel,
        name="block",
        out_shape=(
            jax.ShapeDtypeStruct((tb, dk), bf16),
            jax.ShapeDtypeStruct((tb, dk), bf16),
            jax.ShapeDtypeStruct((dk, f), bf16),
            jax.ShapeDtypeStruct((f, dk), bf16),
        ),
        in_specs=[anywhere] * 4,
        out_specs=(anywhere,) * 4,
        scratch_shapes=[
            vm(n * st, 2 * dk),
            vm(NX, dk, fq),
            vm(NX, fq, dk),
            vm(NX, n * st, 2 * fq),
            vm(NX, n * st, 2 * fq),
            vm(2, n, st, fq),
            vm(2, n, st, 2 * fq),
            vm(n, NX, st // NX, 2 * fq),
            vm(n, NX - 1, st // NX, 2 * fq),
            vm(n * st, 2 * dk),
            vm(n, tb, 2 * dk),
            vm(4, tb, 2 * dk),
        vm(2, tb, 2 * dk),
        vm(2, tb, dk),
            vm(tb, 2 * dk),
            vm(NX, dk, fq),
            vm(NX, fq, dk),
            pltpu.SemaphoreType.DMA((N_SEMS,)),
            pltpu.SemaphoreType.DMA((N_SEMS,)),
            pltpu.SemaphoreType.DMA((24,)),
        ],
        compiler_params=pltpu.CompilerParams(
            collective_id=0, has_side_effects=True, vmem_limit_bytes=56 * 2**20
        ),
        cost_estimate=pl.CostEstimate(flops=12 * n * st * dk * f, bytes_accessed=8 * dk * f, transcendentals=0),
    )(block_input, out_grad, up_weight, down_weight)
    return settle(*results)


def solution(mesh):
    return jax.shard_map(
        body,
        mesh=mesh,
        in_specs=(P("col", "row"), P("col", "row"), P("row", "col"), P("col", "row")),
        out_specs=(P("col", "row"), P("col", "row"), P("row", "col"), P("col", "row")),
        check_vma=False,
    )
```

time: 91.5 us -> 81.1 us (0.89)
  local copies, waits for them, and re-layouts: 7.62 us -> 0 us
  Pallas kernels: 83.1 us -> 80.4 us
    unnamed x6 -> x0, local copies, waits for them, and re-layouts: 7.62 us -> none
    pallas_call x1, Pallas kernels: 83.1 us -> 76 us  [body(): pl.pallas_call(kernel, name='block', out_shape=(jax.ShapeDtypeStruct((tb,...]
    pallas_call x0 -> x1, Pallas kernels: none -> 4.4 us  [settle(): pl.pallas_call(settle_kernel, name='settle', out_shape=tuple((jax.ShapeDt...]
where the time goes in v2:
time: 81.1 us; the launch traced here: 81 us
  Pallas kernels  80.4 us (99%)
    pallas_call x1, Pallas kernels, body(): pl.pallas_call(kernel, name='block', out_shape=(jax.ShapeDtypeStruct((tb,...  76 us
    pallas_call x1, Pallas kernels, settle(): pl.pallas_call(settle_kernel, name='settle', out_shape=tuple((jax.ShapeDt...  4.4 us

profile of v2, /device:TPU:1, one launch (start us, length us, event | category | flops | bytes accessed | tf_op | source)
XLA Modules:
  0.0 81.0 jit_solution(13035011750333556446)
XLA Ops:
  0.6 76.0 %block.1 = (bf16[32,768]{1,0:T(8,128)(2,1)}, bf16[32,768]{1,0:T(8,128)(2,1)}, bf16[768,1536]{1,0:T(8,128)(2,1)}, bf16[1536,768]{1,0:T(8,128)(2,1)}) custom-call(bf16[32,768]{1,0:T(8,128)(2,1)} %x_in.1, bf16[32,768]{1,0:T(8,128)(2,1)} %g_in.1, bf16[768,1536]{1,0:T(8,128)(2,1)} %u_in.1, bf16[1536,768]{1,0:T(8,128)(2,1)} %d_in.1), custom_call_target="tpu_custom_call" | custom-call | flops 7247757312 | bytes 9437184 | tf_op jit(solution)/shard_map/block/pallas_call | solution.py:353
  76.6 4.4 %settle.1 = (bf16[32,768]{1,0:T(8,128)(2,1)}, bf16[32,768]{1,0:T(8,128)(2,1)}, bf16[768,1536]{1,0:T(8,128)(2,1)}, bf16[1536,768]{1,0:T(8,128)(2,1)}) custom-call(bf16[32,768]{1,0:T(8,128)(2,1)} %get-tuple-element.8.refs_0_, bf16[32,768]{1,0:T(8,128)(2,1)} %get-tuple-element.9.refs_1_, bf16[768,1536]{1,0:T(8,128)(2,1)} %get-tuple-element.10.refs_2_, ...), custom_call_target="tpu_custom_call" | custom-call | tf_op jit(solution)/shard_map/settle/pallas_call | solution.py:335

commit v3 on v2

v3 whole, which is shorter than its diff:
```python
import functools

import jax
import jax.numpy as jnp
from jax import lax
from jax.experimental import pallas as pl
from jax.experimental.pallas import tpu as pltpu
from jax.sharding import PartitionSpec as P

MESH = pl.DeviceIdType.MESH
gelu_c = 0.7978845608028654
f32 = jnp.float32
bf16 = jnp.bfloat16

NX = 4
NZ = 8
ORDER = (0, 1, -1, 2, -2, 3, -3, 4)
Y_FIRST = (1, 2, 5, 7)
ZSLOT = {1: 0, -1: 1, 2: 2, -2: 3}
POS = {d: i for i, d in enumerate(ORDER)}
SCHEDULE = (
    ("tr", 0), ("aa", 1), ("aa", -1), ("p1", 0), ("arr", 1), ("arr", -1), ("aa", 2), ("p1", 1),
    ("aa", -2), ("pb", 0), ("arr", 2), ("p1", 2), ("arr", -2), ("s1", 0), ("pb", 2), ("pb", 1),
    ("p1", 3), ("pb", 3), ("s1", 1), ("aa", -3), ("aa", 3), ("p1", 4), ("arr", 3), ("arr", -3),
    ("p1", 5), ("p1", 6), ("s1", 2), ("pb", 6), ("pb", 5), ("arr", 4), ("pb", 4), ("p1", 7),
    ("s1", 6), ("s1", 3), ("s1", 5), ("pb", 7), ("s1", 4), ("s2", 1), ("s1", 7), ("s2", 6),
    ("s2", 5), ("s2", 2), ("s2", 4), ("s2", 3), ("s2", 7), ("s3", 6), ("s2", 0), ("s3", 5),
    ("s3", 1), ("s3", 4), ("s3", 7), ("s3", 3), ("s4", 6), ("s4", 5), ("s4", 4), ("s4", 7),
    ("s5", 6), ("s4", 3), ("s3", 2), ("s5", 5), ("s5", 7), ("s4", 1), ("s5", 4), ("s3", 0),
    ("p2", 6), ("s5", 3), ("p2", 5), ("s6", 6), ("p2", 7), ("s5", 1), ("s6", 7), ("s4", 2),
    ("s6", 5), ("s4", 0), ("p2", 4), ("p2", 1), ("s5", 2), ("p2", 3), ("s6", 1), ("s5", 0),
    ("s6", 4), ("s6", 3), ("p2", 2), ("dw", 0), ("s6", 2), ("p2", 0), ("dw", 1), ("dw", 2),
    ("s6", 0), ("dw", 3),
)
N_SEMS = 224


def activate(preact, hgrad):
    cubed = preact * preact * preact
    tanh_term = jnp.tanh(gelu_c * (preact + 0.044715 * cubed))
    value = 0.5 * preact * (1.0 + tanh_term)
    slope = 0.5 * (1.0 + tanh_term) + 0.5 * preact * (1.0 - tanh_term * tanh_term) * gelu_c * (
        1.0 + 3.0 * 0.044715 * preact * preact
    )
    return value.astype(bf16), (hgrad * slope).astype(bf16)


def dot(a, b, ca, cb):
    return lax.dot_general(a, b, (((ca,), (cb,)), ((), ())), preferred_element_type=f32)


def kernel(
    x_in, g_in, u_in, d_in,
    out_o, back_o, ug_o, dg_o,
    xg, u, dn, ut, dt, part, hid, via, full, quarter, got, outp, sib, zbuf, mid, mid4,
    ssem, rsem, lsem,
):
    tb, dk = x_in.shape
    fq = u.shape[2]
    st = 2 * tb
    sub = st // NX
    row, col = lax.axis_index("row"), lax.axis_index("col")
    cx, cy = row % NX, row // NX
    cz, core = col // 2, col % 2

    def device(axis, off):
        if axis == "x":
            return (cy * NX + (cx + off) % NX, col)
        if axis == "y":
            return (((cy + off) % NX) * NX + cx, col)
        if axis == "z":
            return (row, ((cz + off + NZ) % NZ) * 2 + core)
        return (row, cz * 2 + 1 - core)

    place = {"x": cx, "y": cy}
    sends = []
    n_local = [0]

    def send(src, dst, target):
        i = len(sends)
        copy = pltpu.make_async_remote_copy(
            src_ref=src, dst_ref=dst, send_sem=ssem.at[i], recv_sem=rsem.at[i],
            device_id=target, device_id_type=MESH,
        )
        copy.start()
        sends.append(copy)
        return copy

    def local(src, dst):
        i = n_local[0]
        n_local[0] += 1
        copy = pltpu.make_async_copy(src, dst, lsem.at[i])
        copy.start()
        return copy

    def rows(pos, first=0, count=st):
        return pl.ds(pos * st + first, count)

    own = [
        local(x_in, xg.at[rows(POS[0], 0, tb), pl.ds(0, dk)]),
        local(g_in, xg.at[rows(POS[0], 0, tb), pl.ds(dk, dk)]),
    ]
    weights = [local(u_in.at[:, pl.ds(q * fq, fq)], u.at[q]) for q in range(NX)]
    weights += [local(d_in.at[pl.ds(q * fq, fq), :], dn.at[q]) for q in range(NX)]

    barrier = pltpu.get_barrier_semaphore()
    partners = [(a, o) for a in "xy" for o in (1, 2, 3)] + [("z", o) for o in (1, 2, -1, -2)] + [("c", 1)]
    for axis, off in partners:
        pl.semaphore_signal(barrier, inc=1, device_id=device(axis, off), device_id_type=MESH)
    pl.semaphore_wait(barrier, len(partners))

    arrival, shared = {}, {}

    def pass_on(d, to, half, off):
        cols = pl.ds(half * dk, dk)
        arrival[to, half] = send(
            xg.at[rows(POS[d], 0, tb), cols], xg.at[rows(POS[to], 0, tb), cols], device("z", off)
        )

    def share(d):
        shared[d] = send(xg.at[rows(POS[d], 0, tb)], xg.at[rows(POS[d], tb, tb)], device("c", 1))

    for copy in own:
        copy.wait()
    for half in (0, 1):
        pass_on(0, -1, half, 1)
        pass_on(0, 1, half, -1)
    share(0)

    def arrive(d, half):
        arrival[d, half].wait_recv()
        if d in (-1, -2):
            pass_on(d, d - 1, half, 1)
        elif d in (1, 2):
            pass_on(d, d + 1, half, -1)
        elif (d, half) == (-3, 0):
            pass_on(d, 4, half, 1)
        elif (d, half) == (3, 1):
            pass_on(d, 4, half, -1)

    def arrive_first(d):
        arrive(d, 0)

    def arrive_second(d):
        if d == 4:
            arrive(d, 0)
        arrive(d, 1)
        share(d)

    def turn(_):
        for copy in weights:
            copy.wait()
        for q in range(NX):
            dt[q] = dn[q].T
            ut[q] = u[q].T

    pend, first = {}, {}
    low, high = pl.ds(0, fq), pl.ds(fq, fq)

    def axes(pos):
        return ("y", "x") if pos in Y_FIRST else ("x", "y")

    def around(pos):
        at = place[axes(pos)[0]]
        return at, (at + 1) % NX, (at + 2) % NX, (at + NX - 1) % NX

    def product(pos, q):
        part[q, rows(pos), :fq] = dot(xg[rows(pos), :dk], u[q], 1, 0).astype(bf16)
        part[q, rows(pos), fq:] = dot(xg[rows(pos), dk:], dt[q], 1, 0).astype(bf16)

    def far_products(pos):
        a1, _ = axes(pos)
        _, _, across, _ = around(pos)
        shared[ORDER[pos]].wait_recv()
        product(pos, across)
        first[pos] = [
            send(part.at[across, rows(pos), low], via.at[0, pos], device(a1, 1)),
            send(part.at[across, rows(pos), high], via.at[1, pos], device(a1, -1)),
        ]

    def near_products(pos):
        a1, _ = axes(pos)
        at, right, _, left = around(pos)
        product(pos, right)
        product(pos, left)
        pend[pos] = [
            send(part.at[right, rows(pos), high], full.at[0, pos, :, high], device(a1, 1)),
            send(part.at[left, rows(pos), low], full.at[1, pos, :, low], device(a1, -1)),
        ]
        product(pos, at)

    def first_sum(pos):
        a1, _ = axes(pos)
        _, right, _, left = around(pos)
        first[pos][0].wait_recv()
        part[right, rows(pos), :fq] = (
            part[right, rows(pos), :fq].astype(f32) + via[0, pos].astype(f32)
        ).astype(bf16)
        pend[pos].append(send(part.at[right, rows(pos), low], full.at[0, pos, :, low], device(a1, 1)))
        first[pos][1].wait_recv()
        part[left, rows(pos), fq:] = (
            part[left, rows(pos), fq:].astype(f32) + via[1, pos].astype(f32)
        ).astype(bf16)
        pend[pos].append(send(part.at[left, rows(pos), high], full.at[1, pos, :, high], device(a1, -1)))

    def second_sum(pos):
        a1, a2 = axes(pos)
        for copy in pend[pos]:
            copy.wait_recv()
        total = (
            part[place[a1], rows(pos), :].astype(f32) + full[0, pos].astype(f32) + full[1, pos].astype(f32)
        ).astype(bf16)
        for k in range(NX):
            quarter[pos, k] = total[k * sub:(k + 1) * sub]
        pend[pos] = [
            send(quarter.at[pos, (place[a2] + o) % NX], got.at[pos, o - 1], device(a2, o)) for o in (1, 3, 2)
        ]

    def act(pos):
        a1, a2 = axes(pos)
        for copy in pend[pos]:
            copy.wait_recv()
        total = quarter[pos, place[a2]].astype(f32)
        for o in range(NX - 1):
            total = total + got[pos, o].astype(f32)
        value, grad = activate(total[:, :fq], total[:, fq:])
        mine = pl.ds(pl.multiple_of(pos * st + place[a2] * sub, sub), sub)
        hid[place[a1], mine, :fq] = value
        hid[place[a1], mine, fq:] = grad
        block = hid.at[place[a1], mine]
        pend[pos] = [send(block, block, device(a2, o)) for o in (1, 3, 2)]

    def gather(pos):
        a1, _ = axes(pos)
        for copy in pend[pos]:
            copy.wait_recv()
        h = hid.at[place[a1], rows(pos), low]
        a = hid.at[place[a1], rows(pos), high]
        first[pos] = [send(h, h, device(a1, 1)), send(a, a, device(a1, -1))]
        pend[pos] = [send(a, a, device(a1, 1)), send(h, h, device(a1, -1))]

    def forward(pos):
        a1, _ = axes(pos)
        _, right, _, left = around(pos)
        first[pos][0].wait_recv()
        block = hid.at[left, rows(pos), low]
        pend[pos].append(send(block, block, device(a1, 1)))
        first[pos][1].wait_recv()
        block = hid.at[right, rows(pos), high]
        pend[pos].append(send(block, block, device(a1, -1)))

    whole = set()

    def complete(pos):
        if pos not in whole:
            whole.add(pos)
            for copy in pend[pos]:
                copy.wait_recv()

    def second_products(pos):
        complete(pos)
        out = dot(hid[0, rows(pos), :fq], dn[0], 1, 0)
        for q in range(1, NX):
            out = out + dot(hid[q, rows(pos), :fq], dn[q], 1, 0)
        outp[rows(pos), :dk] = out.astype(bf16)
        back = dot(hid[0, rows(pos), fq:], ut[0], 1, 0)
        for q in range(1, NX):
            back = back + dot(hid[q, rows(pos), fq:], ut[q], 1, 0)
        outp[rows(pos), dk:] = back.astype(bf16)
        pend[pos] = [send(outp.at[rows(pos, tb, tb)], sib.at[pos], device("c", 1))]

    def both_cores(pos):
        pend[pos][0].wait_recv()
        mine = rows(pos, 0, tb)
        total = outp[mine, :].astype(f32) + sib[pos].astype(f32)
        d = ORDER[pos]
        if d in (2, -2):
            side = 0 if d > 0 else 1
            far[3 if d > 0 else -3].wait_recv()
            far[4][side].wait_recv()
            total = total + mid[side].astype(f32)
            cols = slice(side * dk, side * dk + dk)
            outp[mine, :] = total.astype(bf16)
            outp[mine, cols] = (total[:, cols] + mid4[side].astype(f32)).astype(bf16)
        else:
            outp[mine, :] = total.astype(bf16)
        if d in (3, -3):
            far[d] = send(outp.at[mine], mid.at[0 if d > 0 else 1], device("z", d // 3))
        elif d == 4:
            far[4] = [
                send(outp.at[mine, pl.ds(0, dk)], mid4.at[0], device("z", 2)),
                send(outp.at[mine, pl.ds(dk, dk)], mid4.at[1], device("z", -2)),
            ]
        elif d:
            landed[d] = send(outp.at[mine], zbuf.at[ZSLOT[d]], device("z", d))

    far, landed = {}, {}

    def weight_grads(q):
        for pos in range(len(ORDER)):
            complete(pos)
        ug_o[:, q * fq:(q + 1) * fq] = dot(xg[:, :dk], hid[q, :, fq:], 0, 0).astype(bf16)
        dg_o[q * fq:(q + 1) * fq, :] = dot(hid[q, :, :fq], xg[:, dk:], 0, 0).astype(bf16)

    steps = {
        "aa": arrive_first, "arr": arrive_second, "tr": turn, "p1": far_products, "pb": near_products,
        "s1": first_sum, "s2": second_sum, "s3": act, "s4": gather, "s5": forward, "p2": second_products,
        "s6": both_cores, "dw": weight_grads,
    }
    for name, number in SCHEDULE:
        steps[name](number)

    total = outp[rows(POS[0], 0, tb), :].astype(f32)
    for d in (1, -1, 2, -2):
        landed[d].wait_recv()
        total = total + zbuf[ZSLOT[d]].astype(f32)
    out_o[...] = total[:, :dk].astype(bf16)
    back_o[...] = total[:, dk:].astype(bf16)
    for copy in sends:
        copy.wait_send()


def settle_kernel(*refs):
    n = len(refs) // 2
    copies = [pltpu.make_async_copy(refs[i], refs[n + i], refs[-1].at[i]) for i in range(n)]
    for copy in copies:
        copy.start()
    for copy in copies:
        copy.wait()


def settle(*arrays):
    n = len(arrays)
    return pl.pallas_call(
        settle_kernel,
        name="settle",
        out_shape=tuple(jax.ShapeDtypeStruct(a.shape, a.dtype) for a in arrays),
        in_specs=[pl.BlockSpec(memory_space=pltpu.VMEM)] * n,
        out_specs=(pl.BlockSpec(memory_space=pl.ANY),) * n,
        scratch_shapes=[pltpu.SemaphoreType.DMA((n,))],
        compiler_params=pltpu.CompilerParams(vmem_limit_bytes=16 * 2**20),
    )(*arrays)


def body(block_input, out_grad, up_weight, down_weight):
    tb, dk = block_input.shape
    f = up_weight.shape[1]
    fq, st, n = f // NX, 2 * tb, NZ
    vm = lambda *shape: pltpu.VMEM(shape, bf16)
    results = pl.pallas_call(
        kernel,
        name="block",
        out_shape=(vm(tb, dk), vm(tb, dk), vm(dk, f), vm(f, dk)),
        in_specs=[pl.BlockSpec(memory_space=pltpu.HBM)] * 4,
        out_specs=(pl.BlockSpec(memory_space=pltpu.VMEM),) * 4,
        scratch_shapes=[
            vm(n * st, 2 * dk),
            vm(NX, dk, fq),
            vm(NX, fq, dk),
            vm(NX, fq, dk),
            vm(NX, dk, fq),
            vm(NX, n * st, 2 * fq),
            vm(NX, n * st, 2 * fq),
            vm(2, n, st, fq),
            vm(2, n, st, 2 * fq),
            vm(n, NX, st // NX, 2 * fq),
            vm(n, NX - 1, st // NX, 2 * fq),
            vm(n * st, 2 * dk),
            vm(n, tb, 2 * dk),
            vm(4, tb, 2 * dk),
        vm(2, tb, 2 * dk),
        vm(2, tb, dk),
                pltpu.SemaphoreType.DMA((N_SEMS,)),
            pltpu.SemaphoreType.DMA((N_SEMS,)),
            pltpu.SemaphoreType.DMA((10,)),
        ],
        compiler_params=pltpu.CompilerParams(
            collective_id=0, has_side_effects=True, vmem_limit_bytes=40 * 2**20
        ),
        cost_estimate=pl.CostEstimate(flops=12 * n * st * dk * f, bytes_accessed=8 * dk * f, transcendentals=0),
    )(*(pltpu.with_memory_space_constraint(a, pltpu.HBM) for a in (block_input, out_grad, up_weight, down_weight)))
    return settle(*results)


def solution(mesh):
    return jax.shard_map(
        body,
        mesh=mesh,
        in_specs=(P("col", "row"), P("col", "row"), P("row", "col"), P("col", "row")),
        out_specs=(P("col", "row"), P("col", "row"), P("row", "col"), P("col", "row")),
        check_vma=False,
    )
```

time: 81.1 us -> 73.9 us (0.911)
  Pallas kernels: 80.4 us -> 73 us
    pallas_call x1, Pallas kernels: 76 us -> 70.8 us  [body(): pl.pallas_call(kernel, name='block', out_shape=(vm(tb, dk), vm(tb, dk), v...]
    pallas_call x1, Pallas kernels: 4.4 us -> 2.25 us  [settle(): pl.pallas_call(settle_kernel, name='settle', out_shape=tuple((jax.ShapeDt...]
where the time goes in v3:
time: 73.9 us; the launch traced here: 73.8 us
  Pallas kernels  73 us (99%)
  between operations  0.8 us (1%)
    pallas_call x1, Pallas kernels, body(): pl.pallas_call(kernel, name='block', out_shape=(vm(tb, dk), vm(tb, dk), v...  70.8 us
    pallas_call x1, Pallas kernels, settle(): pl.pallas_call(settle_kernel, name='settle', out_shape=tuple((jax.ShapeDt...  2.25 us

profile of v3, /device:TPU:1, one launch (start us, length us, event | category | flops | bytes accessed | tf_op | source)
XLA Modules:
  0.0 73.8 jit_solution(11028369062851811481)
XLA Ops:
  0.6 70.8 %block.1 = (bf16[32,768]{1,0:T(8,128)(2,1)S(1)}, bf16[32,768]{1,0:T(8,128)(2,1)S(1)}, bf16[768,1536]{1,0:T(8,128)(2,1)S(1)}, bf16[1536,768]{1,0:T(8,128)(2,1)S(1)}) custom-call(bf16[32,768]{1,0:T(8,128)(2,1)} %x_in.1, bf16[32,768]{1,0:T(8,128)(2,1)} %g_in.1, bf16[768,1536]{1,0:T(8,128)(2,1)} %u_in.1, bf16[1536,768]{1,0:T(8,128)(2,1)} %d_in.1), custom_call_target="tpu_custom_call" | custom-call | flops 7247757312 | bytes 9437184 | tf_op jit(solution)/shard_map/block/pallas_call | solution.py:350
  71.4 2.3 %settle.1 = (bf16[32,768]{1,0:T(8,128)(2,1)}, bf16[32,768]{1,0:T(8,128)(2,1)}, bf16[768,1536]{1,0:T(8,128)(2,1)}, bf16[1536,768]{1,0:T(8,128)(2,1)}) custom-call(bf16[32,768]{1,0:T(8,128)(2,1)S(1)} %get-tuple-element.8.refs_0_, bf16[32,768]{1,0:T(8,128)(2,1)S(1)} %get-tuple-element.9.refs_1_, bf16[768,1536]{1,0:T(8,128)(2,1)S(1)} %get-tuple-element.10.refs_2_, ...), custom_call_target="tpu_custom_call" | custom-call | tf_op jit(solution)/shard_map/settle/pallas_call | solution.py:334

commit v4 on v3

--- a/solution.py
+++ b/solution.py
@@ -96,6 +96,10 @@
     def rows(pos, first=0, count=st):
         return pl.ds(pos * st + first, count)
 
+    barrier = pltpu.get_barrier_semaphore()
+    partners = [("z", 1), ("z", -1), ("c", 1)] + [(a, o) for a in "xy" for o in (1, 3, 2)] + [("z", 2), ("z", -2)]
+    for axis, off in partners:
+        pl.semaphore_signal(barrier, inc=1, device_id=device(axis, off), device_id_type=MESH)
     own = [
         local(x_in, xg.at[rows(POS[0], 0, tb), pl.ds(0, dk)]),
         local(g_in, xg.at[rows(POS[0], 0, tb), pl.ds(dk, dk)]),
@@ -103,28 +107,23 @@
     weights = [local(u_in.at[:, pl.ds(q * fq, fq)], u.at[q]) for q in range(NX)]
     weights += [local(d_in.at[pl.ds(q * fq, fq), :], dn.at[q]) for q in range(NX)]
 
-    barrier = pltpu.get_barrier_semaphore()
-    partners = [(a, o) for a in "xy" for o in (1, 2, 3)] + [("z", o) for o in (1, 2, -1, -2)] + [("c", 1)]
-    for axis, off in partners:
-        pl.semaphore_signal(barrier, inc=1, device_id=device(axis, off), device_id_type=MESH)
     pl.semaphore_wait(barrier, len(partners))
 
     arrival, shared = {}, {}
 
     def pass_on(d, to, half, off):
         cols = pl.ds(half * dk, dk)
-        arrival[to, half] = send(
-            xg.at[rows(POS[d], 0, tb), cols], xg.at[rows(POS[to], 0, tb), cols], device("z", off)
-        )
+        source = xg.at[rows(POS[d], 0, tb), cols] if d else (x_in, g_in)[half]
+        arrival[to, half] = send(source, xg.at[rows(POS[to], 0, tb), cols], device("z", off))
 
     def share(d):
         shared[d] = send(xg.at[rows(POS[d], 0, tb)], xg.at[rows(POS[d], tb, tb)], device("c", 1))
 
-    for copy in own:
-        copy.wait()
     for half in (0, 1):
         pass_on(0, -1, half, 1)
         pass_on(0, 1, half, -1)
+    for copy in own:
+        copy.wait()
     share(0)
 
     def arrive(d, half):
@@ -213,7 +212,7 @@
         for k in range(NX):
             quarter[pos, k] = total[k * sub:(k + 1) * sub]
         pend[pos] = [
-            send(quarter.at[pos, (place[a2] + o) % NX], got.at[pos, o - 1], device(a2, o)) for o in (1, 3, 2)
+            send(quarter.at[pos, (place[a2] + o) % NX], got.at[pos, o - 1], device(a2, o)) for o in (2, 1, 3)
         ]
 
     def act(pos):
@@ -228,7 +227,7 @@
         hid[place[a1], mine, :fq] = value
         hid[place[a1], mine, fq:] = grad
         block = hid.at[place[a1], mine]
-        pend[pos] = [send(block, block, device(a2, o)) for o in (1, 3, 2)]
+        pend[pos] = [send(block, block, device(a2, o)) for o in (2, 1, 3)]
 
     def gather(pos):
         a1, _ = axes(pos)
@@ -310,13 +309,17 @@
     for name, number in SCHEDULE:
         steps[name](number)
 
+    last = [landed[d] for d in (1, -2, 2, -1)]
+    for copy in sends:
+        if all(copy is not other for other in last):
+            copy.wait_send()
     total = outp[rows(POS[0], 0, tb), :].astype(f32)
-    for d in (1, -1, 2, -2):
+    for d in (1, -2, 2, -1):
         landed[d].wait_recv()
         total = total + zbuf[ZSLOT[d]].astype(f32)
     out_o[...] = total[:, :dk].astype(bf16)
     back_o[...] = total[:, dk:].astype(bf16)
-    for copy in sends:
+    for copy in last:
         copy.wait_send()
 
 

time: 73.9 us -> 73.9 us (level)
  no operation moved by 1% of the time
where the time goes in v4:
time: 73.9 us; the launch traced here: 73.8 us
  Pallas kernels  73 us (99%)
  between operations  0.8 us (1%)
    pallas_call x1, Pallas kernels, body(): pl.pallas_call(kernel, name='block', out_shape=(vm(tb, dk), vm(tb, dk), v...  70.8 us
    pallas_call x1, Pallas kernels, settle(): pl.pallas_call(settle_kernel, name='settle', out_shape=tuple((jax.ShapeDt...  2.25 us

profile of v4, /device:TPU:1, one launch (start us, length us, event | category | flops | bytes accessed | tf_op | source)
XLA Modules:
  0.0 73.8 jit_solution(14075244713795441593)
XLA Ops:
  0.6 70.8 %block.1 = (bf16[32,768]{1,0:T(8,128)(2,1)S(1)}, bf16[32,768]{1,0:T(8,128)(2,1)S(1)}, bf16[768,1536]{1,0:T(8,128)(2,1)S(1)}, bf16[1536,768]{1,0:T(8,128)(2,1)S(1)}) custom-call(bf16[32,768]{1,0:T(8,128)(2,1)} %x_in.1, bf16[32,768]{1,0:T(8,128)(2,1)} %g_in.1, bf16[768,1536]{1,0:T(8,128)(2,1)} %u_in.1, bf16[1536,768]{1,0:T(8,128)(2,1)} %d_in.1), custom_call_target="tpu_custom_call" | custom-call | flops 7247757312 | bytes 9437184 | tf_op jit(solution)/shard_map/block/pallas_call | solution.py:353
  71.4 2.3 %settle.1 = (bf16[32,768]{1,0:T(8,128)(2,1)}, bf16[32,768]{1,0:T(8,128)(2,1)}, bf16[768,1536]{1,0:T(8,128)(2,1)}, bf16[1536,768]{1,0:T(8,128)(2,1)}) custom-call(bf16[32,768]{1,0:T(8,128)(2,1)S(1)} %get-tuple-element.8.refs_0_, bf16[32,768]{1,0:T(8,128)(2,1)S(1)} %get-tuple-element.9.refs_1_, bf16[768,1536]{1,0:T(8,128)(2,1)S(1)} %get-tuple-element.10.refs_2_, ...), custom_call_target="tpu_custom_call" | custom-call | tf_op jit(solution)/shard_map/settle/pallas_call | solution.py:337

commit v5 on v3

--- a/solution.py
+++ b/solution.py
@@ -263,36 +263,37 @@
         for q in range(1, NX):
             out = out + dot(hid[q, rows(pos), :fq], dn[q], 1, 0)
         outp[rows(pos), :dk] = out.astype(bf16)
+        pend[pos] = [send(outp.at[rows(pos, tb, tb), pl.ds(0, dk)], sib.at[pos, :, pl.ds(0, dk)], device("c", 1))]
         back = dot(hid[0, rows(pos), fq:], ut[0], 1, 0)
         for q in range(1, NX):
             back = back + dot(hid[q, rows(pos), fq:], ut[q], 1, 0)
         outp[rows(pos), dk:] = back.astype(bf16)
-        pend[pos] = [send(outp.at[rows(pos, tb, tb)], sib.at[pos], device("c", 1))]
+        pend[pos].append(
+            send(outp.at[rows(pos, tb, tb), pl.ds(dk, dk)], sib.at[pos, :, pl.ds(dk, dk)], device("c", 1))
+        )
 
     def both_cores(pos):
-        pend[pos][0].wait_recv()
         mine = rows(pos, 0, tb)
-        total = outp[mine, :].astype(f32) + sib[pos].astype(f32)
         d = ORDER[pos]
-        if d in (2, -2):
-            side = 0 if d > 0 else 1
-            far[3 if d > 0 else -3].wait_recv()
-            far[4][side].wait_recv()
-            total = total + mid[side].astype(f32)
-            cols = slice(side * dk, side * dk + dk)
-            outp[mine, :] = total.astype(bf16)
-            outp[mine, cols] = (total[:, cols] + mid4[side].astype(f32)).astype(bf16)
-        else:
-            outp[mine, :] = total.astype(bf16)
-        if d in (3, -3):
-            far[d] = send(outp.at[mine], mid.at[0 if d > 0 else 1], device("z", d // 3))
-        elif d == 4:
-            far[4] = [
-                send(outp.at[mine, pl.ds(0, dk)], mid4.at[0], device("z", 2)),
-                send(outp.at[mine, pl.ds(dk, dk)], mid4.at[1], device("z", -2)),
-            ]
-        elif d:
-            landed[d] = send(outp.at[mine], zbuf.at[ZSLOT[d]], device("z", d))
+        side = 0 if d > 0 else 1
+        for half in (0, 1):
+            cols, span = slice(half * dk, half * dk + dk), pl.ds(half * dk, dk)
+            pend[pos][half].wait_recv()
+            total = outp[mine, cols].astype(f32) + sib[pos, :, cols].astype(f32)
+            if d in (2, -2):
+                far[3 if d > 0 else -3][half].wait_recv()
+                total = total + mid[side, :, cols].astype(f32)
+                if half == side:
+                    far[4][side].wait_recv()
+                    total = total + mid4[side].astype(f32)
+            outp[mine, cols] = total.astype(bf16)
+            block = outp.at[mine, span]
+            if d in (3, -3):
+                far.setdefault(d, []).append(send(block, mid.at[side, :, span], device("z", d // 3)))
+            elif d == 4:
+                far.setdefault(d, []).append(send(block, mid4.at[half], device("z", 2 if half == 0 else -2)))
+            elif d:
+                landed.setdefault(d, []).append(send(block, zbuf.at[ZSLOT[d], :, span], device("z", d)))
 
     far, landed = {}, {}
 
@@ -312,7 +313,8 @@
 
     total = outp[rows(POS[0], 0, tb), :].astype(f32)
     for d in (1, -1, 2, -2):
-        landed[d].wait_recv()
+        for copy in landed[d]:
+            copy.wait_recv()
         total = total + zbuf[ZSLOT[d]].astype(f32)
     out_o[...] = total[:, :dk].astype(bf16)
     back_o[...] = total[:, dk:].astype(bf16)

time: 73.9 us -> 76.4 us (1.034)
  Pallas kernels: 73 us -> 75.5 us
    pallas_call x1, Pallas kernels: 70.8 us -> 73.2 us  [body(): pl.pallas_call(kernel, name='block', out_shape=(vm(tb, dk), vm(tb, dk), v...]
where the time goes in v5:
time: 76.4 us; the launch traced here: 76.3 us
  Pallas kernels  75.5 us (99%)
  between operations  0.8 us (1%)
    pallas_call x1, Pallas kernels, body(): pl.pallas_call(kernel, name='block', out_shape=(vm(tb, dk), vm(tb, dk), v...  73.2 us
    pallas_call x1, Pallas kernels, settle(): pl.pallas_call(settle_kernel, name='settle', out_shape=tuple((jax.ShapeDt...  2.25 us

profile of v5, /device:TPU:1, one launch (start us, length us, event | category | flops | bytes accessed | tf_op | source)
XLA Modules:
  0.0 76.3 jit_solution(14581552041316856787)
XLA Ops:
  0.6 73.2 %block.1 = (bf16[32,768]{1,0:T(8,128)(2,1)S(1)}, bf16[32,768]{1,0:T(8,128)(2,1)S(1)}, bf16[768,1536]{1,0:T(8,128)(2,1)S(1)}, bf16[1536,768]{1,0:T(8,128)(2,1)S(1)}) custom-call(bf16[32,768]{1,0:T(8,128)(2,1)} %x_in.1, bf16[32,768]{1,0:T(8,128)(2,1)} %g_in.1, bf16[768,1536]{1,0:T(8,128)(2,1)} %u_in.1, bf16[1536,768]{1,0:T(8,128)(2,1)} %d_in.1), custom_call_target="tpu_custom_call" | custom-call | flops 7247757312 | bytes 9437184 | tf_op jit(solution)/shard_map/block/pallas_call | solution.py:352
  73.9 2.3 %settle.1 = (bf16[32,768]{1,0:T(8,128)(2,1)}, bf16[32,768]{1,0:T(8,128)(2,1)}, bf16[768,1536]{1,0:T(8,128)(2,1)}, bf16[1536,768]{1,0:T(8,128)(2,1)}) custom-call(bf16[32,768]{1,0:T(8,128)(2,1)S(1)} %get-tuple-element.8.refs_0_, bf16[32,768]{1,0:T(8,128)(2,1)S(1)} %get-tuple-element.9.refs_1_, bf16[768,1536]{1,0:T(8,128)(2,1)S(1)} %get-tuple-element.10.refs_2_, ...), custom_call_target="tpu_custom_call" | custom-call | tf_op jit(solution)/shard_map/settle/pallas_call | solution.py:336
